TPU v7x, 128 devices: a whole 4x4x4 slice. The times are simulated.
128 devices in a mesh: dom: 16 (over x, y), sub: 8 (over z, core).
Axes of the slice: x: 4, y: 4, z: 4, core: 2. Of those that a mesh axis runs over, the one named last changes fastest.
Arguments:
- basis: bfloat16 [1048576, 256], P(('dom', 'sub')), may hold values from -100 to 100
- block_part: int32 [8192], P(('dom', 'sub')), may hold values from 0 to 127, as said below
- block_slot: int32 [8192], P(('dom', 'sub')), may hold values from 0 to 127, as said below
- face_slots: int32 [512, 4], P(('dom', 'sub')), may hold values from 0 to 127, as said below
- neighbors: int32 [16384, 3], P(('dom', 'sub')), may hold values from 0 to 159, as said below
- jacobian: bfloat16 [16384, 3, 128, 128], P(('dom', 'sub')), may hold values from -2 to 6
Outputs:
- galerkin: float32 [256, 256], replicated
- lspg: float32 [256, 256], replicated
- applied: bfloat16 [2097152, 256], P(('dom', 'sub'))
Inputs may be any that keep to these rules, and one draw needn't show every extreme that they name: `block_part`: each device's 64 blocks go to 64 different partitions, exactly 1 to each; a quarter of the partitions receive 128 blocks, a quarter 128 // 2, the others 128 // 4. The pairs (block_part, block_slot) are all different. `face_slots`: every entry names a slot of that partition which holds a block. `neighbors`: the first entry of a row is the row's own slot; entries of live slots name a live local slot or a halo entry.
All inputs are finite; a program needn't handle non-finite values.
Results may differ from a plain program's by a relative error of at most 0.0004.
Values may be sent and summed in bfloat16 or wider, within the bound.
A program may use at most 192 MiB of HBM per device.

v0:
```python
import jax
import jax.numpy as jnp
from jax import lax
from jax.sharding import PartitionSpec as P


def padded_2(block, sides, width):
    for axis, dim in sides:
        count = lax.axis_size(axis)
        forward = [(i, i + 1) for i in range(count - 1)]
        forward.append((count - 1, 0))
        backward = [(target, source) for source, target in forward]
        low = lax.ppermute(
            lax.slice_in_dim(block, block.shape[dim] - width, None, axis=dim), axis, forward
        )
        high = lax.ppermute(lax.slice_in_dim(block, 0, width, axis=dim), axis, backward)
        block = jnp.concatenate([low, block, high], axis=dim)
    return block


def body(basis, block_part, block_slot, face_slots, neighbors, jacobian):
    count = block_part.shape[0]
    width = basis.shape[1]
    rows_block = basis.shape[0] // count
    parts_dom = lax.axis_size("dom")
    parts_sub = lax.axis_size("sub")
    partitions = parts_dom * parts_sub
    capacity = neighbors.shape[0]
    pair_slots = capacity // partitions
    faces_group = face_slots.shape[1]
    blocks = basis.reshape(count, rows_block, width)
    indices = jnp.arange(count, dtype=jnp.int32)
    same_target = block_part[:, None] == block_part[None, :]
    earlier = indices[None, :] < indices[:, None]
    rank_here = jnp.sum(jnp.logical_and(same_target, earlier).astype(jnp.int32), axis=1)
    position = block_part * pair_slots + rank_here
    targets = jnp.arange(partitions * pair_slots, dtype=jnp.int32)
    matches = position[None, :] == targets[:, None]
    filled = jnp.any(matches, axis=1)
    picked = jnp.sum(jnp.where(matches, indices[None, :], 0), axis=1)
    outgoing = jnp.where(filled[:, None, None], blocks[picked], jnp.zeros((), jnp.bfloat16))
    out_slots = jnp.where(filled, block_slot[picked], -1)
    incoming, in_slots = (
        lax.all_to_all(outgoing, ("dom", "sub"), split_axis=0, concat_axis=0, tiled=True),
        lax.all_to_all(out_slots, ("dom", "sub"), split_axis=0, concat_axis=0, tiled=True),
    )
    slot_ids = jnp.arange(capacity, dtype=jnp.int32)
    hits = in_slots[None, :] == slot_ids[:, None]
    alive = jnp.any(hits, axis=1)
    source = jnp.sum(jnp.where(hits, targets[None, :], 0), axis=1)
    table = jnp.where(alive[:, None, None], incoming[source], jnp.zeros((), jnp.bfloat16))
    live = alive.astype(jnp.float32)
    faces = table[face_slots.reshape(-1)].reshape(2, 2, faces_group, rows_block, width)
    padded = padded_2(faces, (("dom", 0), ("sub", 1)), 1)
    halo_rows = jnp.stack(
        [
            padded[0, 1],
            padded[0, 2],
            padded[3, 1],
            padded[3, 2],
            padded[1, 0],
            padded[2, 0],
            padded[1, 3],
            padded[2, 3],
        ],
        axis=0,
    )
    full_table = jnp.concatenate(
        [table, halo_rows.reshape(8 * faces_group, rows_block, width)], axis=0
    )
    gathered = full_table[neighbors]
    product = jnp.einsum("snij,snjk->sik", jacobian, gathered, preferred_element_type=jnp.float32)
    applied = (product * live[:, None, None]).astype(jnp.bfloat16)
    flat_basis = table.reshape(capacity * rows_block, width)
    flat_applied = applied.reshape(capacity * rows_block, width)
    contract = (((0,), (0,)), ((), ()))
    galerkin_part = lax.dot_general(
        flat_basis, flat_applied, contract, preferred_element_type=jnp.float32
    )
    lspg_part = lax.dot_general(
        flat_applied, flat_applied, contract, preferred_element_type=jnp.float32
    )
    galerkin_sum, lspg_sum = lax.psum((galerkin_part, lspg_part), ("dom", "sub"))
    total_rows = count * rows_block * partitions
    galerkin = galerkin_sum / total_rows
    lspg = lspg_sum / total_rows
    return (galerkin, lspg, flat_applied)


def solution(mesh):
    in_specs = (
        P(("dom", "sub"), None),
        P(("dom", "sub")),
        P(("dom", "sub")),
        P(("dom", "sub"), None),
        P(("dom", "sub"), None),
        P(("dom", "sub"), None, None, None),
    )
    out_specs = (P(), P(), P(("dom", "sub"), None))
    return jax.shard_map(body, mesh=mesh, in_specs=in_specs, out_specs=out_specs, check_vma=False)
```

profile of v0, /device:TPU:1, one launch (start us, length us, event | category | flops | bytes accessed | tf_op | source)
XLA Modules:
  0.0 421.0 jit_solution(5231389844251891752)
XLA Ops:
  7.2 0.0 copy-start
  7.2 0.9 convert_reduce_fusion
  8.1 0.7 add.47
  8.8 0.1 fusion.20
  8.9 0.1 select_reduce_fusion.1
  9.0 0.7 compare_select_fusion
  9.6 0.1 copy.23
  9.8 0.2 reshape.142
  10.0 0.0 copy-done
  10.0 1.2 gather_fusion
  11.2 0.7 copy.22
  12.0 11.5 %all-to-all-start = ((s32[128,1,1]{2,1,0:T(1,128)}), s32[128,1,1]{2,1,0:T(1,128)S(1)}, u32[]{:S(2)}, u32[]{:S(2)}) async-start(s32[128,1,1]{2,1,0:T(1,128)} %copy.22), calls=%async_computation | async-start | bytes 131072 | tf_op jit(solution)/shard_map/all_to_all | solution.py:45
  23.5 8.9 %gather_fusion.1 = bf16[128,128,256]{2,1,0:T(8,128)(2,1)} fusion(bf16[64,128,256]{2,1,0:T(8,128)(2,1)} %bitcast.75, s32[1024]{0:T(1024)S(1)} %get-tuple-element.10), kind=kCustom, calls=%fused_computation.1 | custom fusion | bytes 16777728 | tf_op jit(solution)/shard_map/gather | solution.py:41
  32.3 7.4 %broadcast_select_fusion = bf16[128,128,256]{2,1,0:T(8,128)(2,1)} fusion(bf16[128,128,256]{2,1,0:T(8,128)(2,1)} %gather_fusion.1, pred[128]{0:T(512)(128)(4,1)S(1)} %fusion.20), kind=kLoop, calls=%fused_computation.12 | loop fusion | flops 4194304 | bytes 16777344 | tf_op jit(solution)/shard_map/jit(_where)/select_n | solution.py:41
  39.7 0.0 all-to-all-done
  39.7 10.2 %all-to-all-start.1 = ((bf16[128,128,256]{2,1,0:T(8,128)(2,1)}), bf16[128,128,256]{2,1,0:T(8,128)(2,1)}, u32[]{:S(2)}, u32[]{:S(2)}) async-start(bf16[128,128,256]{2,1,0:T(8,128)(2,1)} %broadcast_select_fusion), calls=%async_computation.1 | async-start | bytes 16777216 | tf_op jit(solution)/shard_map/all_to_all | solution.py:44
  50.0 0.0 all-reduce.3.cloned.1.call-start
  50.0 0.0 copy-done.4
  50.0 0.1 reshape.104
  50.1 2.4 reduce
  52.5 0.1 select_reduce_fusion
  52.6 0.1 fusion.19
  52.7 99.9 %all-to-all-done.1 = bf16[128,128,256]{2,1,0:T(8,128)(2,1)} async-done(((bf16[128,128,256]{2,1,0:T(8,128)(2,1)}), bf16[128,128,256]{2,1,0:T(8,128)(2,1)}, u32[]{:S(2)}, u32[]{:S(2)}) %all-to-all-start.1) | async-done | bytes 8388640 | tf_op jit(solution)/shard_map/all_to_all | solution.py:44
  152.6 9.9 %gather_fusion.2 = bf16[128,128,256]{2,1,0:T(8,128)(2,1)} fusion(bf16[128,128,256]{2,1,0:T(8,128)(2,1)} %all-to-all-done.1, s32[1024]{0:T(1024)S(1)} %pad_clamp_fusion.2), kind=kCustom, calls=%fused_computation.2 | custom fusion | bytes 16777728 | tf_op jit(solution)/shard_map/gather | solution.py:51
  162.5 7.3 %broadcast_select_fusion.1 = bf16[128,128,256]{2,1,0:T(8,128)(2,1)} fusion(bf16[128,128,256]{2,1,0:T(8,128)(2,1)} %gather_fusion.2, pred[128]{0:T(512)(128)(4,1)S(1)} %fusion.19), kind=kLoop, calls=%fused_computation.13 | loop fusion | flops 4194304 | bytes 16777344 | tf_op jit(solution)/shard_map/jit(_where)/select_n | solution.py:51
  169.9 4.0 gather_fusion.3
  173.9 0.0 copy-start.2
  173.9 0.1 fusion.26
  174.0 1.4 collective-permute-start
  175.3 3.5 collective-permute-start.1
  178.8 10.9 %collective-permute-done = bf16[1,2,4,128,256]{4,3,2,1,0:T(8,128)(2,1)S(1)} collective-permute-done((bf16[1,2,4,128,256]{4,3,2,1,0:T(8,128)(2,1)S(1)}, bf16[1,2,4,128,256]{4,3,2,1,0:T(8,128)(2,1)S(1)}, u32[]{:S(2)}, u32[]{:S(2)}) %collective-permute-start) | collective-permute-done | bytes 524320 | tf_op jit(solution)/shard_map/ppermute | solution.py:13
  189.7 0.0 collective-permute-done.1
  189.7 0.2 pad_maximum_fusion.1
  190.0 0.2 fusion.25
  190.2 4.6 %collective-permute-start.2 = (bf16[4,1,4,128,256]{4,3,2,1,0:T(8,128)(2,1)S(1)}, bf16[4,1,4,128,256]{4,3,2,1,0:T(8,128)(2,1)S(1)}, u32[]{:S(2)}, u32[]{:S(2)}) collective-permute-start(bf16[4,1,4,128,256]{4,3,2,1,0:T(8,128)(2,1)S(1)} %get-tuple-element.6), channel_id=1, source_target_pairs={{0,1},{1,2},{2,3},{3,4},{4,5},{5,6},{6,7},{7,0},{8,9},{9,10},{10,1... | collective-permute-start | bytes 3145736 | tf_op jit(solution)/shard_map/ppermute | solution.py:13
  194.7 0.0 collective-permute-start.3
  194.8 11.6 %collective-permute-done.2 = bf16[4,1,4,128,256]{4,3,2,1,0:T(8,128)(2,1)S(1)} collective-permute-done((bf16[4,1,4,128,256]{4,3,2,1,0:T(8,128)(2,1)S(1)}, bf16[4,1,4,128,256]{4,3,2,1,0:T(8,128)(2,1)S(1)}, u32[]{:S(2)}, u32[]{:S(2)}) %collective-permute-start.2) | collective-permute-done | bytes 1048608 | tf_op jit(solution)/shard_map/ppermute | solution.py:13
  206.5 2.7 collective-permute-done.3
  209.3 6.4 %pad_maximum_fusion = bf16[160,128,256]{2,1,0:T(8,128)(2,1)} fusion(bf16[32,128,256]{2,1,0:T(8,128)(2,1)S(1)} %bitcast.77, bf16[128,128,256]{2,1,0:T(8,128)(2,1)S(1)} %copy-done.2), kind=kLoop, calls=%fused_computation.7 | loop fusion | flops 5242880 | bytes 20971520 | tf_op jit(solution)/shard_map/concatenate | solution.py:68
  215.7 16.9 %gather_fusion.4 = bf16[384,128,256]{2,1,0:T(8,128)(2,1)} fusion(bf16[160,128,256]{2,1,0:T(8,128)(2,1)} %pad_maximum_fusion, s32[1024]{0:T(1024)S(1)} %get-tuple-element.9), kind=kCustom, calls=%fused_computation.4 | custom fusion | bytes 50333184 | tf_op jit(solution)/shard_map/gather | solution.py:71
  232.6 17.8 %fusion = bf16[128,256,128]{1,2,0:T(8,128)(2,1)} fusion(bf16[128,3,128,128]{3,2,1,0:T(8,128)(2,1)} %param.11, bf16[128,3,128,256]{3,2,1,0:T(8,128)(2,1)} %bitcast.73, f32[128]{0:T(128)S(1)} %convert_element_type.17), kind=kOutput, calls=%fused_computation.6 | convolution fusion | flops 3229614080 | bytes 46137856 | tf_op jit(solution)/shard_map/snij,snjk->sik/dot_general | solution.py:72
  250.4 9.0 %fusion.5 = f32[256,256]{1,0:T(8,128)} fusion(bf16[128,128,256]{2,1,0:T(8,128)(2,1)} %broadcast_select_fusion.1, bf16[128,256,128]{1,2,0:T(8,128)(2,1)} %fusion), kind=kOutput, calls=%fused_computation.15 | convolution fusion | flops 2147483648 | bytes 17039360 | tf_op jit(solution)/shard_map/dot_general | solution.py:77
  259.3 0.0 copy-done.3
  259.3 3.1 fusion.8
  262.4 0.0 all-reduce.3.cloned.1.call-update
  262.4 148.4 %all-reduce.3.cloned.1.call-done = (f32[256,256]{1,0:T(8,128)}, f32[256,256]{1,0:T(8,128)}) async-done(((f32[256,256]{1,0:T(8,128)}, f32[256,256]{1,0:T(8,128)}), (f32[256,256]{1,0:T(8,128)}, f32[256,256]{1,0:T(8,128)})) %all-reduce.3.cloned.1.call-update) | async-done | bytes 524304 | tf_op jit(solution)/shard_map/psum | solution.py:83
  410.8 1.7 broadcast_multiply_fusion.1
  412.5 1.7 broadcast_multiply_fusion
  (21 shorter events, 0.2 us)
Async XLA Ops:
  7.2 2.8 copy-start
  12.0 27.8 %all-to-all-start = ((s32[128,1,1]{2,1,0:T(1,128)}), s32[128,1,1]{2,1,0:T(1,128)S(1)}, u32[]{:S(2)}, u32[]{:S(2)}) async-start(s32[128,1,1]{2,1,0:T(1,128)} %copy.22), calls=%async_computation | async-start | bytes 131072 | tf_op jit(solution)/shard_map/all_to_all | solution.py:45
  39.7 10.3 %copy-start.4 = (s32[4,4]{1,0:T(4,128)S(1)}, s32[4,4]{1,0:T(4,128)}, u32[]{:S(2)}) copy-start(s32[4,4]{1,0:T(4,128)} %param.9) | copy-start | bytes 196
  39.7 112.8 %all-to-all-start.1 = ((bf16[128,128,256]{2,1,0:T(8,128)(2,1)}), bf16[128,128,256]{2,1,0:T(8,128)(2,1)}, u32[]{:S(2)}, u32[]{:S(2)}) async-start(bf16[128,128,256]{2,1,0:T(8,128)(2,1)} %broadcast_select_fusion), calls=%async_computation.1 | async-start | bytes 16777216 | tf_op jit(solution)/shard_map/all_to_all | solution.py:44
  50.0 360.8 %all-reduce.3.cloned.1.call-start = ((), (), s32[]{:S(2)}) async-start(), calls=%async_computation.2 | async-start | bytes 1048576 | tf_op jit(solution)/shard_map/psum | solution.py:83
  173.9 35.4 %copy-start.2 = (bf16[128,128,256]{2,1,0:T(8,128)(2,1)S(1)}, bf16[128,128,256]{2,1,0:T(8,128)(2,1)}, u32[]{:S(2)}) copy-start(bf16[128,128,256]{2,1,0:T(8,128)(2,1)} %broadcast_select_fusion.1) | copy-start | bytes 25165828
  174.0 15.7 %collective-permute-start = (bf16[1,2,4,128,256]{4,3,2,1,0:T(8,128)(2,1)S(1)}, bf16[1,2,4,128,256]{4,3,2,1,0:T(8,128)(2,1)S(1)}, u32[]{:S(2)}, u32[]{:S(2)}) collective-permute-start(bf16[1,2,4,128,256]{4,3,2,1,0:T(8,128)(2,1)S(1)} %bitcast.79), channel_id=1, source_target_pairs={{0,8},{8,16},{16,24},{24,32},{32,40},{40,48},{48,56},{56,64},{64,7... | collective-permute-start | bytes 1572872 | tf_op jit(solution)/shard_map/ppermute | solution.py:13
  175.3 14.4 %collective-permute-start.1 = (bf16[1,2,4,128,256]{4,3,2,1,0:T(8,128)(2,1)S(1)}, bf16[1,2,4,128,256]{4,3,2,1,0:T(8,128)(2,1)S(1)}, u32[]{:S(2)}, u32[]{:S(2)}) collective-permute-start(bf16[1,2,4,128,256]{4,3,2,1,0:T(8,128)(2,1)S(1)} %bitcast.78), channel_id=1, source_target_pairs={{8,0},{16,8},{24,16},{32,24},{40,32},{48,40},{56,48},{64,56},{72,6... | collective-permute-start | bytes 1572872 | tf_op jit(solution)/shard_map/ppermute | solution.py:16
  190.2 16.3 %collective-permute-start.2 = (bf16[4,1,4,128,256]{4,3,2,1,0:T(8,128)(2,1)S(1)}, bf16[4,1,4,128,256]{4,3,2,1,0:T(8,128)(2,1)S(1)}, u32[]{:S(2)}, u32[]{:S(2)}) collective-permute-start(bf16[4,1,4,128,256]{4,3,2,1,0:T(8,128)(2,1)S(1)} %get-tuple-element.6), channel_id=1, source_target_pairs={{0,1},{1,2},{2,3},{3,4},{4,5},{5,6},{6,7},{7,0},{8,9},{9,10},{10,1... | collective-permute-start | bytes 3145736 | tf_op jit(solution)/shard_map/ppermute | solution.py:13
  194.7 14.5 %collective-permute-start.3 = (bf16[4,1,4,128,256]{4,3,2,1,0:T(8,128)(2,1)S(1)}, bf16[4,1,4,128,256]{4,3,2,1,0:T(8,128)(2,1)S(1)}, u32[]{:S(2)}, u32[]{:S(2)}) collective-permute-start(bf16[4,1,4,128,256]{4,3,2,1,0:T(8,128)(2,1)S(1)} %get-tuple-element.5), channel_id=1, source_target_pairs={{1,0},{2,1},{3,2},{4,3},{5,4},{6,5},{7,6},{0,7},{9,8},{10,9},{11,1... | collective-permute-start | bytes 3145736 | tf_op jit(solution)/shard_map/ppermute | solution.py:16
  250.4 9.0 %copy-start.3 = (bf16[128,256,128]{1,2,0:T(8,128)(2,1)S(1)}, bf16[128,256,128]{1,2,0:T(8,128)(2,1)}, u32[]{:S(2)}) copy-start(bf16[128,256,128]{1,2,0:T(8,128)(2,1)} %fusion) | copy-start | bytes 25165828
  250.4 163.8 %copy-start.1 = (s32[64]{0:T(128)S(1)}, s32[64]{0:T(128)}, u32[]{:S(2)}) copy-start(s32[64]{0:T(128)} %param.8) | copy-start | bytes 772
Sparse Core Ops, SparseCore 0:
  262.5 148.1 all-reduce.2
where the time goes:
time: 422 us; the launch traced here: 421 us
  waiting for transfers between devices  273 us (65%)
  local copies, waits for them, and re-layouts  42.5 us (10%)
  starting transfers between devices  31.2 us (7%)
  other arithmetic  29.8 us (7%)
  matrix products  29.8 us (7%)
  between operations  14.2 us (3%)
    psum x1, waiting for transfers between devices, body(): lax.psum((galerkin_part, lspg_part), ('dom', 'sub'))  148 us
    all_to_all x1, waiting for transfers between devices, body(): lax.all_to_all(outgoing, ('dom', 'sub'), split_axis=0, concat_axis=0, til...  99.9 us
    ppermute x2, waiting for transfers between devices, padded_2(): lax.ppermute(lax.slice_in_dim(block, block.shape[dim] - width, None, axis...  22.5 us
    dot_general x1, matrix products, body(): jnp.einsum('snij,snjk->sik', jacobian, gathered, preferred_element_type=j...  17.8 us
    gather x1, local copies, waits for them, and re-layouts, body(): gathered = full_table[neighbors]  16.9 us
    all_to_all x1, starting transfers between devices, body(): lax.all_to_all(out_slots, ('dom', 'sub'), split_axis=0, concat_axis=0, ti...  11.5 us
    all_to_all x1, starting transfers between devices, body(): lax.all_to_all(outgoing, ('dom', 'sub'), split_axis=0, concat_axis=0, til...  10.2 us
    gather x1, local copies, waits for them, and re-layouts, body(): incoming[source]  9.93 us
  transfers between devices with their start and end apart: 7, of which 5 were waited for; matrix products, arithmetic and copies ran while one was open for 5% of the time, Pallas kernels for 0%

commit v1 on v0

v1 whole, which is shorter than its diff:
```python
import functools

import jax
import jax.numpy as jnp
from jax import lax
from jax.experimental import pallas as pl
from jax.experimental.pallas import tpu as pltpu
from jax.sharding import PartitionSpec as P

MESH = pl.DeviceIdType.MESH
BF16 = jnp.bfloat16
F32 = jnp.float32
I32 = jnp.int32

SLABS = ((48, 48, 32), (32, 48, 48))
ORDERS = ((0, 1, 2), (1, 2, 0), (2, 0, 1))
FACES = 4
GL_SLOTS = 4


def offsets(h):
    out, at = [], 0
    for rows in SLABS[h]:
        out.append(at)
        at += rows
    return out


def kernel(
    total_rows,
    part_ref,
    slot_ref,
    face_ref,
    near_ref,
    basis_hbm,
    jac_hbm,
    gal_ref,
    lspg_ref,
    out_hbm,
    basis,
    jac,
    send0, send1, send2, send3, send4, send5,
    one0, one1, one2, one3, one4, one5,
    two0, two1, two2, two3, two4, two5,
    tab0, tab1, tab2, tab3, tab4, tab5,
    face_out0, face_out1,
    halo0, halo1,
    meta,
    ints_v,
    ints_s,
    acc,
    core_in,
    pieces,
    plane_in,
    line_in,
    final,
    in_sem,
    out_sem,
    move_sem,
    local_sem,
):
    send = ((send0, send1, send2), (send3, send4, send5))
    one = ((one0, one1, one2), (one3, one4, one5))
    two = ((two0, two1, two2), (two3, two4, two5))
    tab = ((tab0, tab1, tab2), (tab3, tab4, tab5))
    face_out = (face_out0, face_out1)
    halo = (halo0, halo1)

    dom = lax.axis_index("dom")
    sub = lax.axis_index("sub")
    me = (dom // 4, dom % 4, sub // 2)
    core = sub % 2
    rank = dom * 8 + sub

    def device(shift, flip):
        x, y, z = [(a + b) % 4 for a, b in zip(me, shift)]
        return (x * 4 + y, z * 2 + (core + flip) % 2)

    def along(dim, step):
        shift = [0, 0, 0]
        shift[dim] = step
        return tuple(shift)

    def remote(src, dst, s_sem, r_sem, shift, flip):
        pltpu.make_async_remote_copy(
            src, dst, out_sem.at[s_sem], in_sem.at[r_sem],
            device_id=device(shift, flip), device_id_type=MESH,
        ).start()

    def local(src, dst, r_sem):
        pltpu.make_async_copy(src, dst, in_sem.at[r_sem]).start()

    def landed(view, r_sem):
        pltpu.make_async_copy(view, view, in_sem.at[r_sem]).wait()

    def sent(view, s_sem):
        pltpu.make_async_copy(view, view, out_sem.at[s_sem]).wait()

    basis_copy = pltpu.make_async_copy(basis_hbm, basis, move_sem.at[0])
    basis_copy.start()
    jac_copy = pltpu.make_async_copy(jac_hbm, jac, move_sem.at[1])
    jac_copy.start()

    peers = [((0, 0, 0), 1)]
    for dim in range(3):
        for step in (1, 2, 3):
            peers += [(along(dim, step), 0), (along(dim, step), 1)]
    for dx in (1, 2, 3):
        for dy in (1, 2, 3):
            peers.append(((dx, dy, 0), 0))
    barrier = pltpu.get_barrier_semaphore()
    for shift, flip in peers:
        pl.semaphore_signal(barrier, inc=1, device_id=device(shift, flip), device_id_type=MESH)

    lanes = lax.broadcasted_iota(I32, (1, 128), 1)

    def pick(b, carry):
        index, slot = carry
        hit = lanes == part_ref[b]
        return jnp.where(hit, b, index), jnp.where(hit, slot_ref[b], slot)

    index_row, slot_row = lax.fori_loop(
        0, 64, pick, (jnp.zeros((1, 128), I32), jnp.full((1, 128), -1, I32)), unroll=8
    )
    ints_v[0:1, :] = index_row
    mine = sub
    meta[me[0], me[1], mine] = slot_row
    ints_copy = pltpu.make_async_copy(ints_v, ints_s, local_sem.at[0])
    ints_copy.start()
    for h in range(2):
        for k in range(3):
            tab[h][k][128] = jnp.zeros(tab[h][k].shape[1:], BF16)
        halo[h][32] = jnp.zeros(halo[h].shape[1:], BF16)
    ints_copy.wait()
    basis_copy.wait()
    pl.semaphore_wait(barrier, len(peers))

    META_IN, META_OUT = 18, 18
    for step in (1, 2, 3):
        view = meta.at[me[0], me[1], mine]
        remote(view, view, META_OUT, META_IN, along(0, step), 0)

    def gather(h):
        base = offsets(h)

        def one_block(p, carry):
            block = basis[ints_s[0, p], :, h * 128:(h + 1) * 128]
            to = (p // 32, (p // 8) % 4, (p // 2) % 4)
            for k, (d1, d2, d3) in enumerate(ORDERS):
                rows = SLABS[h][k]
                send[h][k][to[d1] * 4 + to[d2], to[d3] * 2 + p % 2] = block[base[k]:base[k] + rows]
            return carry

        lax.fori_loop(0, 128, one_block, 0, unroll=4)

    def in_id(h, stage, k):
        return (h * 3 + stage) * 3 + k

    def stage1(h):
        for step in (1, 2, 3, 0):
            for k, (d1, d2, d3) in enumerate(ORDERS):
                to = (me[d1] + step) % 4
                src = send[h][k].at[pl.ds(to * 4, 4)]
                dst = one[h][k].at[me[d1]]
                if step:
                    remote(src, dst, in_id(h, 0, k), in_id(h, 0, k), along(d1, step), 0)
                else:
                    local(src, dst, in_id(h, 0, k))

    def stage2(h):
        for k, (d1, d2, d3) in enumerate(ORDERS):
            landed(one[h][k], in_id(h, 0, k))
            for step in (1, 2, 3, 0):
                to = (me[d2] + step) % 4
                src = one[h][k].at[:, to]
                dst = two[h][k].at[pl.ds(me[d2] * 4, 4)]
                if step:
                    remote(src, dst, in_id(h, 1, k), in_id(h, 1, k), along(d2, step), 0)
                else:
                    local(src, dst, in_id(h, 1, k))

    def stage3(h):
        for k, (d1, d2, d3) in enumerate(ORDERS):
            landed(two[h][k], in_id(h, 1, k))
            at = me[d3] * 2 + core
            dst = tab[h][k].at[pl.ds(at * 16, 16)]
            for step in (1, 2, 3, 0):
                for flip in (0, 1):
                    to = (me[d3] + step) % 4 * 2 + (core + flip) % 2
                    src = two[h][k].at[:, to]
                    if step or flip:
                        remote(src, dst, in_id(h, 2, k), in_id(h, 2, k), along(d3, step), flip)
                    else:
                        local(src, dst, in_id(h, 2, k))

    gather(0)
    stage1(0)
    gather(1)
    stage1(1)

    landed(meta.at[pl.ds(0, 3), 0, 0], META_IN)
    for step in (1, 2, 3):
        view = meta.at[:, me[1], mine]
        remote(view, view, META_OUT + 1, META_IN + 1, along(1, step), 0)
    stage2(0)
    stage2(1)
    landed(meta.at[pl.ds(0, 3), :, 0], META_IN + 1)
    for step in (0, 1, 2, 3):
        for flip in (0, 1):
            if step or flip:
                view = meta.at[:, :, mine]
                remote(view, view, META_OUT + 2, META_IN + 2, along(2, step), flip)
    stage3(0)
    stage3(1)

    landed(meta.at[:, :, pl.ds(0, 7)], META_IN + 2)
    arrived = meta[...].reshape(128, 1, 128)
    mine_only = lax.broadcasted_iota(I32, (128, 1, 128), 2) == rank
    slot_of = jnp.sum(jnp.where(mine_only, arrived, 0), axis=2, keepdims=True)
    hit = slot_of == lax.broadcasted_iota(I32, (128, 1, 128), 2)
    source = lax.broadcasted_iota(I32, (128, 1, 128), 0)
    from_ = (source // 32, (source // 8) % 4, (source // 2) % 4)
    for k, (d1, d2, d3) in enumerate(ORDERS):
        place = (from_[d3] * 2 + source % 2) * 16 + from_[d2] * 4 + from_[d1]
        ints_v[1 + k:2 + k, :] = jnp.max(jnp.where(hit, place, 0), axis=0)
    ints_v[4:5, :] = jnp.max(jnp.where(hit, 1, 0), axis=0)
    ints_copy = pltpu.make_async_copy(ints_v, ints_s, local_sem.at[0])
    ints_copy.start()
    ints_copy.wait()

    def table(h, slot):
        return jnp.concatenate([tab[h][k][ints_s[1 + k, slot]] for k in range(3)], axis=0)

    def entry(h, index):
        away = index >= 128
        slot = jnp.minimum(index, 127)
        slabs = [
            tab[h][k][jnp.where(away, 128, ints_s[1 + k, slot])] for k in range(3)
        ]
        near = jnp.concatenate(slabs, axis=0)
        return near + halo[h][jnp.where(away, index - 128, 32)]

    HALO_IN, HALO_OUT = 21, 21

    def send_faces(h):
        for k in range(3):
            landed(tab[h][k].at[pl.ds(0, 128)], in_id(h, 2, k))

        def one_face(e, carry):
            face_out[h][e] = table(h, face_ref[e])
            return carry

        lax.fori_loop(0, 4 * FACES, one_face, 0, unroll=2)
        dom_up = (((dom + 1) % 16), sub)
        dom_down = (((dom + 15) % 16), sub)
        sub_up = (dom, (sub + 1) % 8)
        sub_down = (dom, (sub + 7) % 8)
        moves = (
            (8, 8, 0, dom_up),
            (0, 8, 8, dom_down),
            (4, 4, 16, sub_up),
            (12, 4, 20, sub_up),
            (0, 4, 24, sub_down),
            (8, 4, 28, sub_down),
        )
        for src, count, dst, to in moves:
            pltpu.make_async_remote_copy(
                face_out[h].at[pl.ds(src, count)], halo[h].at[pl.ds(dst, count)],
                out_sem.at[HALO_OUT + h], in_sem.at[HALO_IN + h],
                device_id=to, device_id_type=MESH,
            ).start()

    def apply(h):
        landed(halo[h].at[pl.ds(0, 32)], HALO_IN + h)
        base = offsets(h)

        def one_slot(s, carry):
            own = table(h, s)
            first = entry(h, near_ref[s * 3 + 1])
            second = entry(h, near_ref[s * 3 + 2])
            right = jnp.concatenate([own, first, second], axis=0)
            left = jnp.concatenate([jac[s, 0], jac[s, 1], jac[s, 2]], axis=1)
            product = jnp.dot(left, right, preferred_element_type=F32)
            rows = (product * ints_s[4, s].astype(F32)).astype(BF16)
            for k in range(3):
                send[h][k][s // 8, s % 8] = rows[base[k]:base[k] + SLABS[h][k]]
            return carry

        lax.fori_loop(0, 128, one_slot, 0, unroll=4)
        for k in range(3):
            rows = SLABS[h][k]
            pltpu.make_async_copy(
                send[h][k],
                out_hbm.at[:, :, pl.ds(base[k], rows), pl.ds(h * 128, 128)],
                move_sem.at[2 + h * 3 + k],
            ).start()

    def stage1_sent(h):
        for k in range(3):
            sent(one[h][k].at[pl.ds(0, 3)], in_id(h, 0, k))

    send_faces(0)
    jac_copy.wait()
    stage1_sent(0)
    apply(0)
    send_faces(1)
    stage1_sent(1)
    apply(1)

    acc[...] = jnp.zeros_like(acc)

    def grams(g, carry):
        columns = []
        for h in range(2):
            columns.append(jnp.concatenate(
                [table(h, g * GL_SLOTS + e) for e in range(GL_SLOTS)], axis=0))
        for h in range(2):
            columns.append(jnp.concatenate(
                [send[h][k][(g * GL_SLOTS + e) // 8, (g * GL_SLOTS + e) % 8]
                 for e in range(GL_SLOTS) for k in range(3)], axis=0))
        basis_rows = jnp.concatenate(columns[:2], axis=1)
        rows = jnp.concatenate(columns[2:], axis=1)
        contract = (((0,), (0,)), ((), ()))
        acc[0] += lax.dot_general(basis_rows, rows, contract, preferred_element_type=F32)
        acc[1] += lax.dot_general(rows, rows, contract, preferred_element_type=F32)
        return carry

    lax.fori_loop(0, 128 // GL_SLOTS, grams, 0)

    SUM_IN, SUM_OUT = 23, 23
    other = ((0, 0, 0), 1)
    remote(acc.at[1 - core], core_in, SUM_OUT, SUM_IN, *other)
    landed(core_in, SUM_IN)
    pieces[...] = (acc[core] + core_in[...]).reshape(16, 16, 256)
    planes = [(dx, dy, 0) for dx in range(4) for dy in range(4) if dx or dy]
    for dx, dy, dz in planes:
        to = (me[0] + dx) % 4 * 4 + (me[1] + dy) % 4
        remote(pieces.at[to], plane_in.at[dom], SUM_OUT + 1, SUM_IN + 1, (dx, dy, 0), 0)
    plane_in[dom] = pieces[dom]
    landed(plane_in.at[pl.ds(0, 15)], SUM_IN + 1)
    line_in[me[2]] = jnp.sum(plane_in[...], axis=0)
    for step in (1, 2, 3):
        view = line_in.at[me[2]]
        remote(view, view, SUM_OUT + 2, SUM_IN + 2, along(2, step), 0)
    landed(line_in.at[pl.ds(0, 3)], SUM_IN + 2)
    final[core, dom] = jnp.sum(line_in[...], axis=0) * (1.0 / total_rows)
    for dx, dy, dz in planes:
        view = final.at[core, dom]
        remote(view, view, SUM_OUT + 3, SUM_IN + 3, (dx, dy, 0), 0)
    landed(final.at[0, pl.ds(0, 15)], SUM_IN + 3)
    remote(final.at[core], final.at[core], SUM_OUT + 4, SUM_IN + 4, *other)
    landed(final.at[0], SUM_IN + 4)
    gal_ref[...] = final[0].reshape(256, 256)
    lspg_ref[...] = final[1].reshape(256, 256)

    for h in range(2):
        for k in range(3):
            sent(two[h][k].at[pl.ds(0, 12)], in_id(h, 1, k))
            sent(tab[h][k].at[pl.ds(0, 112)], in_id(h, 2, k))
        sent(halo[h].at[pl.ds(0, 32)], HALO_OUT + h)
    sent(meta.at[pl.ds(0, 3), 0, 0], META_OUT)
    sent(meta.at[pl.ds(0, 3), :, 0], META_OUT + 1)
    sent(meta.at[:, :, pl.ds(0, 7)], META_OUT + 2)
    sent(core_in, SUM_OUT)
    sent(plane_in.at[pl.ds(0, 15)], SUM_OUT + 1)
    sent(line_in.at[pl.ds(0, 3)], SUM_OUT + 2)
    sent(final.at[0, pl.ds(0, 15)], SUM_OUT + 3)
    sent(final.at[0], SUM_OUT + 4)
    for h in range(2):
        base = offsets(h)
        for k in range(3):
            pltpu.make_async_copy(
                send[h][k],
                out_hbm.at[:, :, pl.ds(base[k], SLABS[h][k]), pl.ds(h * 128, 128)],
                move_sem.at[2 + h * 3 + k],
            ).wait()


def body(basis, block_part, block_slot, face_slots, neighbors, jacobian):
    total_rows = 128 * basis.shape[0]
    blocks = basis.reshape(64, 128, 256)
    slabs = [(h, k) for h in range(2) for k in range(3)]
    scratch = [pltpu.VMEM((64, 128, 256), BF16), pltpu.VMEM((128, 3, 128, 128), BF16)]
    scratch += [pltpu.VMEM((16, 8, SLABS[h][k], 128), BF16) for h, k in slabs]
    scratch += [pltpu.VMEM((4, 4, 8, SLABS[h][k], 128), BF16) for h, k in slabs]
    scratch += [pltpu.VMEM((16, 8, SLABS[h][k], 128), BF16) for h, k in slabs]
    scratch += [pltpu.VMEM((129, SLABS[h][k], 128), BF16) for h, k in slabs]
    scratch += [pltpu.VMEM((16, 128, 128), BF16)] * 2
    scratch += [pltpu.VMEM((33, 128, 128), BF16)] * 2
    scratch += [
        pltpu.VMEM((4, 4, 8, 1, 128), I32),
        pltpu.VMEM((8, 128), I32),
        pltpu.SMEM((8, 128), I32),
        pltpu.VMEM((2, 256, 256), F32),
        pltpu.VMEM((256, 256), F32),
        pltpu.VMEM((16, 16, 256), F32),
        pltpu.VMEM((16, 16, 256), F32),
        pltpu.VMEM((4, 16, 256), F32),
        pltpu.VMEM((2, 16, 16, 256), F32),
        pltpu.SemaphoreType.DMA((28,)),
        pltpu.SemaphoreType.DMA((28,)),
        pltpu.SemaphoreType.DMA((8,)),
        pltpu.SemaphoreType.DMA((1,)),
    ]
    smem = pl.BlockSpec(memory_space=pltpu.SMEM)
    vmem = pl.BlockSpec(memory_space=pltpu.VMEM)
    anywhere = pl.BlockSpec(memory_space=pl.ANY)
    galerkin, lspg, applied = pl.pallas_call(
        functools.partial(kernel, total_rows),
        out_shape=(
            jax.ShapeDtypeStruct((256, 256), F32),
            jax.ShapeDtypeStruct((256, 256), F32),
            jax.ShapeDtypeStruct((16, 8, 128, 256), BF16),
        ),
        in_specs=[smem, smem, smem, smem, anywhere, anywhere],
        out_specs=(vmem, vmem, anywhere),
        scratch_shapes=scratch,
        compiler_params=pltpu.CompilerParams(
            collective_id=0, has_side_effects=True, vmem_limit_bytes=60 * 2**20
        ),
        cost_estimate=pl.CostEstimate(
            flops=7_500_000_000, bytes_accessed=25_000_000, transcendentals=0
        ),
        name="regroup_apply_reduce",
    )(block_part, block_slot, face_slots.reshape(-1), neighbors.reshape(-1), blocks, jacobian)
    return galerkin, lspg, applied.reshape(16384, 256)


def solution(mesh):
    in_specs = (
        P(("dom", "sub"), None),
        P(("dom", "sub")),
        P(("dom", "sub")),
        P(("dom", "sub"), None),
        P(("dom", "sub"), None),
        P(("dom", "sub"), None, None, None),
    )
    out_specs = (P(), P(), P(("dom", "sub"), None))
    return jax.shard_map(body, mesh=mesh, in_specs=in_specs, out_specs=out_specs, check_vma=False)
```

time: 422 us -> 185 us (0.44)
  waiting for transfers between devices: 273 us -> 0 us
  Pallas kernels: 0 us -> 171 us
  starting transfers between devices: 31.2 us -> 0 us
  matrix products: 29.8 us -> 0 us
  other arithmetic: 29.8 us -> 0 us
  local copies, waits for them, and re-layouts: 42.5 us -> 13.3 us
  between operations: 14.2 us -> 0.64 us
    pallas_call x0 -> x1, Pallas kernels: none -> 171 us  [body(): pl.pallas_call(functools.partial(kernel, total_rows), out_shape=(jax.Shap...]
    psum x1 -> x0, waiting for transfers between devices: 148 us -> none  [body(): lax.psum((galerkin_part, lspg_part), ('dom', 'sub'))]
    all_to_all x2 -> x0, waiting for transfers between devices: 99.9 us -> none  [the longest x1 99.9 us: body(): lax.all_to_all(outgoing, ('dom', 'sub'), split_axis=0, concat_axis=0, til...]
    gather x5 -> x0, local copies, waits for them, and re-layouts: 40.9 us -> none  [the longest x1 16.9 us: body(): gathered = full_table[neighbors]]
    dot_general x3 -> x0, matrix products: 29.8 us -> none  [the longest x1 17.8 us: body(): jnp.einsum('snij,snjk->sik', jacobian, gathered, preferred_element_type=j...]
    ppermute x4 -> x0, waiting for transfers between devices: 25.2 us -> none  [the longest x2 22.5 us: padded_2(): lax.ppermute(lax.slice_in_dim(block, block.shape[dim] - width, None, axis...]
    all_to_all x2 -> x0, starting transfers between devices: 21.7 us -> none  [the longest x1 11.5 us: body(): lax.all_to_all(out_slots, ('dom', 'sub'), split_axis=0, concat_axis=0, ti...]
    select_n x7 -> x0, other arithmetic: 15.5 us -> none  [the longest x1 7.41 us: body(): jnp.where(filled[:, None, None], blocks[picked], jnp.zeros((), jnp.bfloat...]
  transfers between devices with their start and end apart: 7 -> 0, of which waited for: 5 -> 0; matrix products, arithmetic and copies ran while one was open for 5% -> 0% of each run, Pallas kernels for 0% -> 0%
where the time goes in v1:
time: 185 us; the launch traced here: 184 us
  Pallas kernels  171 us (92%)
  local copies, waits for them, and re-layouts  13.3 us (7%)
    pallas_call x1, Pallas kernels, body(): pl.pallas_call(functools.partial(kernel, total_rows), out_shape=(jax.Shap...  171 us
    unnamed x4, local copies, waits for them, and re-layouts  11.2 us

profile of v1, /device:TPU:1, one launch (start us, length us, event | category | flops | bytes accessed | tf_op | source)
XLA Modules:
  0.0 184.4 jit_solution(5953808318435378887)
XLA Ops:
  0.6 1.3 reshape.18.face_ref
  1.9 0.8 copy.9
  2.7 0.8 reshape.19.near_ref
  3.5 170.5 %regroup_apply_reduce.1 = (f32[256,256]{1,0:T(8,128)}, f32[256,256]{1,0:T(8,128)}, bf16[16,8,128,256]{3,2,1,0:T(8,128)(2,1)}) custom-call(s32[64]{0:T(128)} %part_ref.1, s32[64]{0:T(128)} %slot_ref.1, s32[16]{0:T(128)} %reshape.18.face_ref, s32[384]{0:T(512)} %reshape.19.near_ref, bf16[64,128,256]{2,1,0:T(8,128)(2,1)} %bitcast.3, ...), custom_call_target="tpu_custom_call" | custom-call | flops 7500000256 | bytes 25000000 | tf_op jit(solution)/shard_map/regroup_apply_reduce/pallas_call | solution.py:408
  174.0 1.7 copy.13
  175.7 1.7 copy.14
  177.3 7.1 %copy.15 = bf16[16384,256]{1,0:T(8,128)(2,1)} copy(bf16[16384,256]{1,0:T(8,128)(2,1)} %bitcast.2) | data formatting | bytes 16777216

commit v2 on v1

--- a/solution.py
+++ b/solution.py
@@ -12,10 +12,13 @@
 F32 = jnp.float32
 I32 = jnp.int32
 
-SLABS = ((48, 48, 32), (32, 48, 48))
+SLABS = ((48, 32, 48), (48, 48, 32))
 ORDERS = ((0, 1, 2), (1, 2, 0), (2, 0, 1))
 FACES = 4
-GL_SLOTS = 4
+BATCH = 16
+BEFORE = 3
+EARLY = ((1, 0), (3, 0), (1, 1), (3, 1))
+LATE = ((2, 0), (2, 1), (0, 1), (0, 0))
 
 
 def offsets(h):
@@ -36,10 +39,9 @@
     jac_hbm,
     gal_ref,
     lspg_ref,
-    out_hbm,
+    out_ref,
     basis,
     jac,
-    send0, send1, send2, send3, send4, send5,
     one0, one1, one2, one3, one4, one5,
     two0, two1, two2, two3, two4, two5,
     tab0, tab1, tab2, tab3, tab4, tab5,
@@ -59,7 +61,6 @@
     move_sem,
     local_sem,
 ):
-    send = ((send0, send1, send2), (send3, send4, send5))
     one = ((one0, one1, one2), (one3, one4, one5))
     two = ((two0, two1, two2), (two3, two4, two5))
     tab = ((tab0, tab1, tab2), (tab3, tab4, tab5))
@@ -148,7 +149,8 @@
             to = (p // 32, (p // 8) % 4, (p // 2) % 4)
             for k, (d1, d2, d3) in enumerate(ORDERS):
                 rows = SLABS[h][k]
-                send[h][k][to[d1] * 4 + to[d2], to[d3] * 2 + p % 2] = block[base[k]:base[k] + rows]
+                out_ref[to[d1] * 4 + to[d2], to[d3] * 2 + p % 2, base[k]:base[k] + rows,
+                        h * 128:(h + 1) * 128] = block[base[k]:base[k] + rows]
             return carry
 
         lax.fori_loop(0, 128, one_block, 0, unroll=4)
@@ -156,62 +158,66 @@
     def in_id(h, stage, k):
         return (h * 3 + stage) * 3 + k
 
-    def stage1(h):
+    def stage1(h, k):
+        d1, d2, d3 = ORDERS[k]
         for step in (1, 2, 3, 0):
-            for k, (d1, d2, d3) in enumerate(ORDERS):
-                to = (me[d1] + step) % 4
-                src = send[h][k].at[pl.ds(to * 4, 4)]
-                dst = one[h][k].at[me[d1]]
-                if step:
-                    remote(src, dst, in_id(h, 0, k), in_id(h, 0, k), along(d1, step), 0)
-                else:
-                    local(src, dst, in_id(h, 0, k))
-
-    def stage2(h):
-        for k, (d1, d2, d3) in enumerate(ORDERS):
+            to = (me[d1] + step) % 4
+            src = out_ref.at[
+                pl.ds(to * 4, 4), :, pl.ds(offsets(h)[k], SLABS[h][k]), pl.ds(h * 128, 128)]
+            dst = one[h][k].at[me[d1]]
+            if step:
+                remote(src, dst, in_id(h, 0, k), in_id(h, 0, k), along(d1, step), 0)
+            else:
+                local(src, dst, in_id(h, 0, k))
+
+    def stage2(h, k):
+        d1, d2, d3 = ORDERS[k]
+        for step in (1, 2, 3, 0):
+            to = (me[d2] + step) % 4
+            src = one[h][k].at[:, to]
+            dst = two[h][k].at[pl.ds(me[d2] * 4, 4)]
+            if step:
+                remote(src, dst, in_id(h, 1, k), in_id(h, 1, k), along(d2, step), 0)
+            else:
+                local(src, dst, in_id(h, 1, k))
+
+    def stage3(h, k, moves):
+        d1, d2, d3 = ORDERS[k]
+        dst = tab[h][k].at[pl.ds((me[d3] * 2 + core) * 16, 16)]
+        for step, flip in moves:
+            to = (me[d3] + step) % 4 * 2 + (core + flip) % 2
+            src = two[h][k].at[:, to]
+            if step or flip:
+                remote(src, dst, in_id(h, 2, k), in_id(h, 2, k), along(d3, step), flip)
+            else:
+                local(src, dst, in_id(h, 2, k))
+
+    gather(0)
+    for k in range(3):
+        stage1(0, k)
+    gather(1)
+    for k in range(3):
+        stage1(1, k)
+    for h in range(2):
+        for k in range(3):
             landed(one[h][k], in_id(h, 0, k))
-            for step in (1, 2, 3, 0):
-                to = (me[d2] + step) % 4
-                src = one[h][k].at[:, to]
-                dst = two[h][k].at[pl.ds(me[d2] * 4, 4)]
-                if step:
-                    remote(src, dst, in_id(h, 1, k), in_id(h, 1, k), along(d2, step), 0)
-                else:
-                    local(src, dst, in_id(h, 1, k))
-
-    def stage3(h):
-        for k, (d1, d2, d3) in enumerate(ORDERS):
-            landed(two[h][k], in_id(h, 1, k))
-            at = me[d3] * 2 + core
-            dst = tab[h][k].at[pl.ds(at * 16, 16)]
-            for step in (1, 2, 3, 0):
-                for flip in (0, 1):
-                    to = (me[d3] + step) % 4 * 2 + (core + flip) % 2
-                    src = two[h][k].at[:, to]
-                    if step or flip:
-                        remote(src, dst, in_id(h, 2, k), in_id(h, 2, k), along(d3, step), flip)
-                    else:
-                        local(src, dst, in_id(h, 2, k))
-
-    gather(0)
-    stage1(0)
-    gather(1)
-    stage1(1)
-
+            stage2(h, k)
     landed(meta.at[pl.ds(0, 3), 0, 0], META_IN)
     for step in (1, 2, 3):
         view = meta.at[:, me[1], mine]
         remote(view, view, META_OUT + 1, META_IN + 1, along(1, step), 0)
-    stage2(0)
-    stage2(1)
+    for k in range(3):
+        landed(two[0][k], in_id(0, 1, k))
+        stage3(0, k, EARLY + LATE)
     landed(meta.at[pl.ds(0, 3), :, 0], META_IN + 1)
     for step in (0, 1, 2, 3):
         for flip in (0, 1):
             if step or flip:
                 view = meta.at[:, :, mine]
                 remote(view, view, META_OUT + 2, META_IN + 2, along(2, step), flip)
-    stage3(0)
-    stage3(1)
+    for k in range(3):
+        landed(two[1][k], in_id(1, 1, k))
+        stage3(1, k, EARLY)
 
     landed(meta.at[:, :, pl.ds(0, 7)], META_IN + 2)
     arrived = meta[...].reshape(128, 1, 128)
@@ -247,7 +253,7 @@
             landed(tab[h][k].at[pl.ds(0, 128)], in_id(h, 2, k))
 
         def one_face(e, carry):
-            face_out[h][e] = table(h, face_ref[e])
+            face_out[h][e] = table(h, face_ref[e // FACES, e % FACES])
             return carry
 
         lax.fori_loop(0, 4 * FACES, one_face, 0, unroll=2)
@@ -270,62 +276,68 @@
                 device_id=to, device_id_type=MESH,
             ).start()
 
-    def apply(h):
-        landed(halo[h].at[pl.ds(0, 32)], HALO_IN + h)
-        base = offsets(h)
-
-        def one_slot(s, carry):
-            own = table(h, s)
-            first = entry(h, near_ref[s * 3 + 1])
-            second = entry(h, near_ref[s * 3 + 2])
-            right = jnp.concatenate([own, first, second], axis=0)
-            left = jnp.concatenate([jac[s, 0], jac[s, 1], jac[s, 2]], axis=1)
-            product = jnp.dot(left, right, preferred_element_type=F32)
-            rows = (product * ints_s[4, s].astype(F32)).astype(BF16)
-            for k in range(3):
-                send[h][k][s // 8, s % 8] = rows[base[k]:base[k] + SLABS[h][k]]
+    contract = (((0,), (0,)), ((), ()))
+
+    def tables(h, first):
+        return jnp.concatenate([table(h, first + e) for e in range(BATCH)], axis=0)
+
+    def applied(h, g):
+        per = BATCH // 8
+        rows = out_ref[pl.ds(g * per, per), :, :, h * 128:(h + 1) * 128]
+        return rows.reshape(BATCH * 128, 128)
+
+    def apply(h, low, high):
+        def some_slots(g, carry):
+            done = []
+            for e in range(BATCH):
+                s = g * BATCH + e
+                right = jnp.concatenate(
+                    [table(h, s), entry(h, near_ref[1, s]), entry(h, near_ref[2, s])], axis=0)
+                left = jnp.concatenate([jac[s, 0], jac[s, 1], jac[s, 2]], axis=1)
+                product = jnp.dot(left, right, preferred_element_type=F32)
+                rows = (product * ints_s[4, s].astype(F32)).astype(BF16)
+                out_ref[s // 8, s % 8, :, h * 128:(h + 1) * 128] = rows
+                done.append(rows)
+            rows = jnp.concatenate(done, axis=0)
+            first = g * BATCH
+            if h == 0:
+                right = jnp.concatenate([tables(0, first), rows], axis=1)
+                gram = lax.dot_general(rows, right, contract, preferred_element_type=F32)
+                acc[0, :128, :128] += gram[:, :128]
+                acc[1, :128, :128] += gram[:, 128:]
+            else:
+                right = jnp.concatenate(
+                    [tables(0, first), tables(1, first), applied(0, g), rows], axis=1)
+                gram = lax.dot_general(rows, right, contract, preferred_element_type=F32)
+                acc[0, 128:, :] += gram[:, :256]
+                acc[1, 128:, :] += gram[:, 256:]
             return carry
 
-        lax.fori_loop(0, 128, one_slot, 0, unroll=4)
-        for k in range(3):
-            rows = SLABS[h][k]
-            pltpu.make_async_copy(
-                send[h][k],
-                out_hbm.at[:, :, pl.ds(base[k], rows), pl.ds(h * 128, 128)],
-                move_sem.at[2 + h * 3 + k],
-            ).start()
-
-    def stage1_sent(h):
+        lax.fori_loop(low, high, some_slots, 0)
+
+    def gram_across():
+        def some_slots(g, carry):
+            acc[0, :128, 128:] += lax.dot_general(
+                applied(0, g), tables(1, g * BATCH), contract, preferred_element_type=F32)
+            return carry
+
+        lax.fori_loop(0, 128 // BATCH, some_slots, 0)
+
+    acc[...] = jnp.zeros_like(acc)
+    send_faces(0)
+    for k in range(3):
+        stage3(1, k, LATE)
+    for h in range(2):
         for k in range(3):
             sent(one[h][k].at[pl.ds(0, 3)], in_id(h, 0, k))
-
-    send_faces(0)
     jac_copy.wait()
-    stage1_sent(0)
-    apply(0)
+    landed(halo[0].at[pl.ds(0, 32)], HALO_IN)
+    apply(0, 0, BEFORE)
     send_faces(1)
-    stage1_sent(1)
-    apply(1)
-
-    acc[...] = jnp.zeros_like(acc)
-
-    def grams(g, carry):
-        columns = []
-        for h in range(2):
-            columns.append(jnp.concatenate(
-                [table(h, g * GL_SLOTS + e) for e in range(GL_SLOTS)], axis=0))
-        for h in range(2):
-            columns.append(jnp.concatenate(
-                [send[h][k][(g * GL_SLOTS + e) // 8, (g * GL_SLOTS + e) % 8]
-                 for e in range(GL_SLOTS) for k in range(3)], axis=0))
-        basis_rows = jnp.concatenate(columns[:2], axis=1)
-        rows = jnp.concatenate(columns[2:], axis=1)
-        contract = (((0,), (0,)), ((), ()))
-        acc[0] += lax.dot_general(basis_rows, rows, contract, preferred_element_type=F32)
-        acc[1] += lax.dot_general(rows, rows, contract, preferred_element_type=F32)
-        return carry
-
-    lax.fori_loop(0, 128 // GL_SLOTS, grams, 0)
+    apply(0, BEFORE, 128 // BATCH)
+    gram_across()
+    landed(halo[1].at[pl.ds(0, 32)], HALO_IN + 1)
+    apply(1, 0, 128 // BATCH)
 
     SUM_IN, SUM_OUT = 23, 23
     other = ((0, 0, 0), 1)
@@ -344,14 +356,20 @@
         remote(view, view, SUM_OUT + 2, SUM_IN + 2, along(2, step), 0)
     landed(line_in.at[pl.ds(0, 3)], SUM_IN + 2)
     final[core, dom] = jnp.sum(line_in[...], axis=0) * (1.0 / total_rows)
-    for dx, dy, dz in planes:
-        view = final.at[core, dom]
-        remote(view, view, SUM_OUT + 3, SUM_IN + 3, (dx, dy, 0), 0)
-    landed(final.at[0, pl.ds(0, 15)], SUM_IN + 3)
-    remote(final.at[core], final.at[core], SUM_OUT + 4, SUM_IN + 4, *other)
-    landed(final.at[0], SUM_IN + 4)
-    gal_ref[...] = final[0].reshape(256, 256)
-    lspg_ref[...] = final[1].reshape(256, 256)
+    view = final.at[core, dom]
+    for n, (dx, dy, dz) in enumerate(planes):
+        remote(view, view, SUM_OUT + 3, SUM_IN + 4 + n, (dx, dy, 0), 0)
+    remote(view, view, SUM_OUT + 4, SUM_IN + 3, *other)
+    for n, (dx, dy, dz) in enumerate(planes):
+        view = final.at[core, (me[0] - dx) % 4 * 4 + (me[1] - dy) % 4]
+        landed(view, SUM_IN + 4 + n)
+        remote(view, view, SUM_OUT + 4, SUM_IN + 3, *other)
+    landed(final.at[0], SUM_IN + 3)
+    flipped = final[0].reshape(256, 256)
+    lower = final[1].reshape(256, 256)
+    gal_ref[...] = flipped.T
+    lspg_ref[...] = lower
+    lspg_ref[:128, 128:] = lower[128:, :128].T
 
     for h in range(2):
         for k in range(3):
@@ -366,14 +384,6 @@
     sent(line_in.at[pl.ds(0, 3)], SUM_OUT + 2)
     sent(final.at[0, pl.ds(0, 15)], SUM_OUT + 3)
     sent(final.at[0], SUM_OUT + 4)
-    for h in range(2):
-        base = offsets(h)
-        for k in range(3):
-            pltpu.make_async_copy(
-                send[h][k],
-                out_hbm.at[:, :, pl.ds(base[k], SLABS[h][k]), pl.ds(h * 128, 128)],
-                move_sem.at[2 + h * 3 + k],
-            ).wait()
 
 
 def body(basis, block_part, block_slot, face_slots, neighbors, jacobian):
@@ -381,7 +391,6 @@
     blocks = basis.reshape(64, 128, 256)
     slabs = [(h, k) for h in range(2) for k in range(3)]
     scratch = [pltpu.VMEM((64, 128, 256), BF16), pltpu.VMEM((128, 3, 128, 128), BF16)]
-    scratch += [pltpu.VMEM((16, 8, SLABS[h][k], 128), BF16) for h, k in slabs]
     scratch += [pltpu.VMEM((4, 4, 8, SLABS[h][k], 128), BF16) for h, k in slabs]
     scratch += [pltpu.VMEM((16, 8, SLABS[h][k], 128), BF16) for h, k in slabs]
     scratch += [pltpu.VMEM((129, SLABS[h][k], 128), BF16) for h, k in slabs]
@@ -397,9 +406,9 @@
         pltpu.VMEM((16, 16, 256), F32),
         pltpu.VMEM((4, 16, 256), F32),
         pltpu.VMEM((2, 16, 16, 256), F32),
+        pltpu.SemaphoreType.DMA((42,)),
         pltpu.SemaphoreType.DMA((28,)),
-        pltpu.SemaphoreType.DMA((28,)),
-        pltpu.SemaphoreType.DMA((8,)),
+        pltpu.SemaphoreType.DMA((2,)),
         pltpu.SemaphoreType.DMA((1,)),
     ]
     smem = pl.BlockSpec(memory_space=pltpu.SMEM)
@@ -408,21 +417,21 @@
     galerkin, lspg, applied = pl.pallas_call(
         functools.partial(kernel, total_rows),
         out_shape=(
-            jax.ShapeDtypeStruct((256, 256), F32),
-            jax.ShapeDtypeStruct((256, 256), F32),
-            jax.ShapeDtypeStruct((16, 8, 128, 256), BF16),
+            pltpu.VMEM((256, 256), F32),
+            pltpu.VMEM((256, 256), F32),
+            pltpu.VMEM((16, 8, 128, 256), BF16),
         ),
         in_specs=[smem, smem, smem, smem, anywhere, anywhere],
-        out_specs=(vmem, vmem, anywhere),
+        out_specs=(vmem, vmem, vmem),
         scratch_shapes=scratch,
         compiler_params=pltpu.CompilerParams(
-            collective_id=0, has_side_effects=True, vmem_limit_bytes=60 * 2**20
+            collective_id=0, has_side_effects=True, vmem_limit_bytes=54 * 2**20
         ),
         cost_estimate=pl.CostEstimate(
             flops=7_500_000_000, bytes_accessed=25_000_000, transcendentals=0
         ),
         name="regroup_apply_reduce",
-    )(block_part, block_slot, face_slots.reshape(-1), neighbors.reshape(-1), blocks, jacobian)
+    )(block_part, block_slot, face_slots, neighbors.T, blocks, jacobian)
     return galerkin, lspg, applied.reshape(16384, 256)
 
 

time: 185 us -> 154 us (0.83)
  Pallas kernels: 171 us -> 149 us
  local copies, waits for them, and re-layouts: 13.3 us -> 4.8 us
    pallas_call x1, Pallas kernels: 171 us -> 149 us  [body(): pl.pallas_call(functools.partial(kernel, total_rows), out_shape=(pltpu.VM...]
    unnamed x4 -> x3, local copies, waits for them, and re-layouts: 11.2 us -> 4.8 us
    reshape x2 -> x0, local copies, waits for them, and re-layouts: 2.06 us -> none  [the longest x1 1.27 us: body(): face_slots.reshape(-1)]
where the time goes in v2:
time: 154 us
  Pallas kernels  149 us (97%)
  local copies, waits for them, and re-layouts  4.8 us (3%)
    pallas_call x1, Pallas kernels, body(): pl.pallas_call(functools.partial(kernel, total_rows), out_shape=(pltpu.VM...  149 us
    unnamed x3, local copies, waits for them, and re-layouts  4.8 us

profile of v2, /device:TPU:1, one launch (start us, length us, event | category | flops | bytes accessed | tf_op | source)
XLA Modules:
  0.0 154.0 jit_solution(6976085814503188793)
XLA Ops:
  0.6 148.5 %regroup_apply_reduce.1 = (f32[256,256]{1,0:T(8,128)S(1)}, f32[256,256]{1,0:T(8,128)S(1)}, bf16[16,8,128,256]{3,2,1,0:T(8,128)(2,1)S(1)}) custom-call(s32[64]{0:T(128)} %part_ref.1, s32[64]{0:T(128)} %slot_ref.1, s32[4,4]{1,0:T(4,128)} %face_ref.1, s32[3,128]{1,0:T(4,128)} %bitcast.5, bf16[64,128,256]{2,1,0:T(8,128)(2,1)} %bitcast.4, ...), custom_call_target="tpu_custom_call" | custom-call | flops 7500000256 | bytes 25000000 | tf_op jit(solution)/shard_map/regroup_apply_reduce/pallas_call | solution.py:417
  149.2 0.7 copy.12
  149.9 0.7 copy.13
  150.6 3.4 %copy.14 = bf16[16384,256]{1,0:T(8,128)(2,1)} copy(bf16[16384,256]{1,0:T(8,128)(2,1)S(1)} %bitcast.3) | data formatting | bytes 16777216

commit v3 on v2

--- a/solution.py
+++ b/solution.py
@@ -15,7 +15,8 @@
 SLABS = ((48, 32, 48), (48, 48, 32))
 ORDERS = ((0, 1, 2), (1, 2, 0), (2, 0, 1))
 FACES = 4
-BATCH = 16
+PARTS = 4
+BATCH = 32
 BEFORE = 3
 EARLY = ((1, 0), (3, 0), (1, 1), (3, 1))
 LATE = ((2, 0), (2, 1), (0, 1), (0, 0))
@@ -100,7 +101,6 @@
     basis_copy = pltpu.make_async_copy(basis_hbm, basis, move_sem.at[0])
     basis_copy.start()
     jac_copy = pltpu.make_async_copy(jac_hbm, jac, move_sem.at[1])
-    jac_copy.start()
 
     peers = [((0, 0, 0), 1)]
     for dim in range(3):
@@ -134,12 +134,7 @@
         halo[h][32] = jnp.zeros(halo[h].shape[1:], BF16)
     ints_copy.wait()
     basis_copy.wait()
-    pl.semaphore_wait(barrier, len(peers))
-
-    META_IN, META_OUT = 18, 18
-    for step in (1, 2, 3):
-        view = meta.at[me[0], me[1], mine]
-        remote(view, view, META_OUT, META_IN, along(0, step), 0)
+    jac_copy.start()
 
     def gather(h):
         base = offsets(h)
@@ -193,10 +188,17 @@
                 local(src, dst, in_id(h, 2, k))
 
     gather(0)
-    for k in range(3):
+    pl.semaphore_wait(barrier, len(peers))
+
+    META_IN, META_OUT = 18, 18
+    for step in (1, 2, 3):
+        view = meta.at[me[0], me[1], mine]
+        remote(view, view, META_OUT, META_IN, along(0, step), 0)
+
+    for k in (1, 0, 2):
         stage1(0, k)
     gather(1)
-    for k in range(3):
+    for k in (1, 0, 2):
         stage1(1, k)
     for h in range(2):
         for k in range(3):
@@ -206,7 +208,7 @@
     for step in (1, 2, 3):
         view = meta.at[:, me[1], mine]
         remote(view, view, META_OUT + 1, META_IN + 1, along(1, step), 0)
-    for k in range(3):
+    for k in (2, 0, 1):
         landed(two[0][k], in_id(0, 1, k))
         stage3(0, k, EARLY + LATE)
     landed(meta.at[pl.ds(0, 3), :, 0], META_IN + 1)
@@ -215,7 +217,7 @@
             if step or flip:
                 view = meta.at[:, :, mine]
                 remote(view, view, META_OUT + 2, META_IN + 2, along(2, step), flip)
-    for k in range(3):
+    for k in (2, 0, 1):
         landed(two[1][k], in_id(1, 1, k))
         stage3(1, k, EARLY)
 
@@ -325,7 +327,7 @@
 
     acc[...] = jnp.zeros_like(acc)
     send_faces(0)
-    for k in range(3):
+    for k in (2, 0, 1):
         stage3(1, k, LATE)
     for h in range(2):
         for k in range(3):
@@ -344,7 +346,7 @@
     remote(acc.at[1 - core], core_in, SUM_OUT, SUM_IN, *other)
     landed(core_in, SUM_IN)
     pieces[...] = (acc[core] + core_in[...]).reshape(16, 16, 256)
-    planes = [(dx, dy, 0) for dx in range(4) for dy in range(4) if dx or dy]
+    planes = [(dx, dy, 0) for dx in (2, 1, 3, 0) for dy in (2, 1, 3, 0) if dx or dy]
     for dx, dy, dz in planes:
         to = (me[0] + dx) % 4 * 4 + (me[1] + dy) % 4
         remote(pieces.at[to], plane_in.at[dom], SUM_OUT + 1, SUM_IN + 1, (dx, dy, 0), 0)
@@ -384,6 +386,20 @@
     sent(line_in.at[pl.ds(0, 3)], SUM_OUT + 2)
     sent(final.at[0, pl.ds(0, 15)], SUM_OUT + 3)
     sent(final.at[0], SUM_OUT + 4)
+
+
+def deliver(*refs):
+    sources, results, sem = refs[:3], refs[3:6], refs[6]
+    moves = []
+    for n in range(PARTS):
+        rows = pl.ds(n * (16 // PARTS), 16 // PARTS)
+        moves.append((sources[2].at[rows], results[2].at[rows]))
+    moves += [(sources[0], results[0]), (sources[1], results[1])]
+    copies = [pltpu.make_async_copy(a, b, sem.at[n]) for n, (a, b) in enumerate(moves)]
+    for copy in copies:
+        copy.start()
+    for copy in copies:
+        copy.wait()
 
 
 def body(basis, block_part, block_slot, face_slots, neighbors, jacobian):
@@ -432,6 +448,20 @@
         ),
         name="regroup_apply_reduce",
     )(block_part, block_slot, face_slots, neighbors.T, blocks, jacobian)
+    galerkin, lspg, applied = pl.pallas_call(
+        deliver,
+        out_shape=(
+            jax.ShapeDtypeStruct((256, 256), F32),
+            jax.ShapeDtypeStruct((256, 256), F32),
+            jax.ShapeDtypeStruct((16, 8, 128, 256), BF16),
+        ),
+        in_specs=[vmem, vmem, vmem],
+        out_specs=(anywhere, anywhere, anywhere),
+        scratch_shapes=[pltpu.SemaphoreType.DMA((PARTS + 2,))],
+        compiler_params=pltpu.CompilerParams(vmem_limit_bytes=16 * 2**20),
+        cost_estimate=pl.CostEstimate(flops=0, bytes_accessed=17_800_000, transcendentals=0),
+        name="deliver",
+    )(galerkin, lspg, applied)
     return galerkin, lspg, applied.reshape(16384, 256)
 
 

time: 154 us -> 149 us (0.968)
  local copies, waits for them, and re-layouts: 4.8 us -> 0 us
    unnamed x3 -> x0, local copies, waits for them, and re-layouts: 4.8 us -> none
    pallas_call x0 -> x1, Pallas kernels: none -> 3.48 us  [body(): pl.pallas_call(deliver, out_shape=(jax.ShapeDtypeStruct((256, 256), F32),...]
    pallas_call x1, Pallas kernels: 149 us -> 145 us  [body(): pl.pallas_call(functools.partial(kernel, total_rows), out_shape=(pltpu.VM...]
where the time goes in v3:
time: 149 us
  Pallas kernels  149 us (100%)
    pallas_call x1, Pallas kernels, body(): pl.pallas_call(functools.partial(kernel, total_rows), out_shape=(pltpu.VM...  145 us
    pallas_call x1, Pallas kernels, body(): pl.pallas_call(deliver, out_shape=(jax.ShapeDtypeStruct((256, 256), F32),...  3.48 us

profile of v3, /device:TPU:1, one launch (start us, length us, event | category | flops | bytes accessed | tf_op | source)
XLA Modules:
  0.0 149.3 jit_solution(15629899474595726573)
XLA Ops:
  0.6 145.2 %regroup_apply_reduce.1 = (f32[256,256]{1,0:T(8,128)S(1)}, f32[256,256]{1,0:T(8,128)S(1)}, bf16[16,8,128,256]{3,2,1,0:T(8,128)(2,1)S(1)}) custom-call(s32[64]{0:T(128)} %part_ref.1, s32[64]{0:T(128)} %slot_ref.1, s32[4,4]{1,0:T(4,128)} %face_ref.1, s32[3,128]{1,0:T(4,128)} %bitcast.5, bf16[64,128,256]{2,1,0:T(8,128)(2,1)} %bitcast.4, ...), custom_call_target="tpu_custom_call" | custom-call | flops 7500000256 | bytes 25000000 | tf_op jit(solution)/shard_map/regroup_apply_reduce/pallas_call | solution.py:433
  145.8 3.5 %deliver.1 = (f32[256,256]{1,0:T(8,128)}, f32[256,256]{1,0:T(8,128)}, bf16[16,8,128,256]{3,2,1,0:T(8,128)(2,1)}) custom-call(f32[256,256]{1,0:T(8,128)S(1)} %get-tuple-element.9.refs_0_, f32[256,256]{1,0:T(8,128)S(1)} %get-tuple-element.10.refs_1_, bf16[16,8,128,256]{3,2,1,0:T(8,128)(2,1)S(1)} %get-tuple-element.11.refs_2_), custom_call_target="tpu_custom_call" | custom-call | bytes 17800000 | tf_op jit(solution)/shard_map/deliver/pallas_call | solution.py:451

commit v4 on v3

--- a/solution.py
+++ b/solution.py
@@ -12,9 +12,10 @@
 F32 = jnp.float32
 I32 = jnp.int32
 
-SLABS = ((48, 32, 48), (48, 48, 32))
+SLABS = ((48, 48, 32), (48, 48, 32))
 ORDERS = ((0, 1, 2), (1, 2, 0), (2, 0, 1))
 FACES = 4
+FAR = (2, 1, 3, 0)
 PARTS = 4
 BATCH = 32
 BEFORE = 3
@@ -54,8 +55,7 @@
     acc,
     core_in,
     pieces,
-    plane_in,
-    line_in,
+    cube_in,
     final,
     in_sem,
     out_sem,
@@ -106,9 +106,8 @@
     for dim in range(3):
         for step in (1, 2, 3):
             peers += [(along(dim, step), 0), (along(dim, step), 1)]
-    for dx in (1, 2, 3):
-        for dy in (1, 2, 3):
-            peers.append(((dx, dy, 0), 0))
+    cube = [(dx, dy, dz) for dx in FAR for dy in FAR for dz in FAR if dx or dy or dz]
+    peers += [(shift, 0) for shift in cube if (shift, 0) not in peers]
     barrier = pltpu.get_barrier_semaphore()
     for shift, flip in peers:
         pl.semaphore_signal(barrier, inc=1, device_id=device(shift, flip), device_id_type=MESH)
@@ -305,21 +304,21 @@
             if h == 0:
                 right = jnp.concatenate([tables(0, first), rows], axis=1)
                 gram = lax.dot_general(rows, right, contract, preferred_element_type=F32)
-                acc[0, :128, :128] += gram[:, :128]
-                acc[1, :128, :128] += gram[:, 128:]
+                acc[0, 0, :128] += gram[:, :128]
+                acc[1, 0, :128] += gram[:, 128:]
             else:
                 right = jnp.concatenate(
                     [tables(0, first), tables(1, first), applied(0, g), rows], axis=1)
                 gram = lax.dot_general(rows, right, contract, preferred_element_type=F32)
-                acc[0, 128:, :] += gram[:, :256]
-                acc[1, 128:, :] += gram[:, 256:]
+                for n in range(4):
+                    acc[n // 2, n % 2, 128:] += gram[:, n * 128:(n + 1) * 128]
             return carry
 
         lax.fori_loop(low, high, some_slots, 0)
 
     def gram_across():
         def some_slots(g, carry):
-            acc[0, :128, 128:] += lax.dot_general(
+            acc[0, 1, :128] += lax.dot_general(
                 applied(0, g), tables(1, g * BATCH), contract, preferred_element_type=F32)
             return carry
 
@@ -345,33 +344,27 @@
     other = ((0, 0, 0), 1)
     remote(acc.at[1 - core], core_in, SUM_OUT, SUM_IN, *other)
     landed(core_in, SUM_IN)
-    pieces[...] = (acc[core] + core_in[...]).reshape(16, 16, 256)
-    planes = [(dx, dy, 0) for dx in (2, 1, 3, 0) for dy in (2, 1, 3, 0) if dx or dy]
-    for dx, dy, dz in planes:
-        to = (me[0] + dx) % 4 * 4 + (me[1] + dy) % 4
-        remote(pieces.at[to], plane_in.at[dom], SUM_OUT + 1, SUM_IN + 1, (dx, dy, 0), 0)
-    plane_in[dom] = pieces[dom]
-    landed(plane_in.at[pl.ds(0, 15)], SUM_IN + 1)
-    line_in[me[2]] = jnp.sum(plane_in[...], axis=0)
-    for step in (1, 2, 3):
-        view = line_in.at[me[2]]
-        remote(view, view, SUM_OUT + 2, SUM_IN + 2, along(2, step), 0)
-    landed(line_in.at[pl.ds(0, 3)], SUM_IN + 2)
-    final[core, dom] = jnp.sum(line_in[...], axis=0) * (1.0 / total_rows)
-    view = final.at[core, dom]
-    for n, (dx, dy, dz) in enumerate(planes):
-        remote(view, view, SUM_OUT + 3, SUM_IN + 4 + n, (dx, dy, 0), 0)
-    remote(view, view, SUM_OUT + 4, SUM_IN + 3, *other)
-    for n, (dx, dy, dz) in enumerate(planes):
-        view = final.at[core, (me[0] - dx) % 4 * 4 + (me[1] - dy) % 4]
-        landed(view, SUM_IN + 4 + n)
-        remote(view, view, SUM_OUT + 4, SUM_IN + 3, *other)
+    pieces[...] = (acc[core] + core_in[...]).reshape(64, 8, 128)
+    chip = dom * 4 + me[2]
+    for dx, dy, dz in cube:
+        to = ((me[0] + dx) % 4 * 4 + (me[1] + dy) % 4) * 4 + (me[2] + dz) % 4
+        remote(pieces.at[to], cube_in.at[chip], SUM_OUT + 1, SUM_IN + 1, (dx, dy, dz), 0)
+    cube_in[chip] = pieces[chip]
+    landed(cube_in.at[pl.ds(0, 63)], SUM_IN + 1)
+    final[core, chip] = jnp.sum(cube_in[...], axis=0) * (1.0 / total_rows)
+    view = final.at[core, chip]
+    for shift in cube:
+        remote(view, view, SUM_OUT + 2, SUM_IN + 2, shift, 0)
+    landed(final.at[0, pl.ds(0, 63)], SUM_IN + 2)
+    remote(final.at[core], final.at[core], SUM_OUT + 3, SUM_IN + 3, *other)
     landed(final.at[0], SUM_IN + 3)
-    flipped = final[0].reshape(256, 256)
-    lower = final[1].reshape(256, 256)
-    gal_ref[...] = flipped.T
-    lspg_ref[...] = lower
-    lspg_ref[:128, 128:] = lower[128:, :128].T
+    flipped = final[0].reshape(2, 256, 128)
+    lower = final[1].reshape(2, 256, 128)
+    gal_ref[:128, :] = flipped[0].T
+    gal_ref[128:, :] = flipped[1].T
+    lspg_ref[:, :128] = lower[0]
+    lspg_ref[:128, 128:] = lower[0, 128:].T
+    lspg_ref[128:, 128:] = lower[1, 128:]
 
     for h in range(2):
         for k in range(3):
@@ -382,10 +375,9 @@
     sent(meta.at[pl.ds(0, 3), :, 0], META_OUT + 1)
     sent(meta.at[:, :, pl.ds(0, 7)], META_OUT + 2)
     sent(core_in, SUM_OUT)
-    sent(plane_in.at[pl.ds(0, 15)], SUM_OUT + 1)
-    sent(line_in.at[pl.ds(0, 3)], SUM_OUT + 2)
-    sent(final.at[0, pl.ds(0, 15)], SUM_OUT + 3)
-    sent(final.at[0], SUM_OUT + 4)
+    sent(cube_in.at[pl.ds(0, 63)], SUM_OUT + 1)
+    sent(final.at[0, pl.ds(0, 63)], SUM_OUT + 2)
+    sent(final.at[0], SUM_OUT + 3)
 
 
 def deliver(*refs):
@@ -416,13 +408,12 @@
         pltpu.VMEM((4, 4, 8, 1, 128), I32),
         pltpu.VMEM((8, 128), I32),
         pltpu.SMEM((8, 128), I32),
-        pltpu.VMEM((2, 256, 256), F32),
-        pltpu.VMEM((256, 256), F32),
-        pltpu.VMEM((16, 16, 256), F32),
-        pltpu.VMEM((16, 16, 256), F32),
-        pltpu.VMEM((4, 16, 256), F32),
-        pltpu.VMEM((2, 16, 16, 256), F32),
-        pltpu.SemaphoreType.DMA((42,)),
+        pltpu.VMEM((2, 2, 256, 128), F32),
+        pltpu.VMEM((2, 256, 128), F32),
+        pltpu.VMEM((64, 8, 128), F32),
+        pltpu.VMEM((64, 8, 128), F32),
+        pltpu.VMEM((2, 64, 8, 128), F32),
+        pltpu.SemaphoreType.DMA((28,)),
         pltpu.SemaphoreType.DMA((28,)),
         pltpu.SemaphoreType.DMA((2,)),
         pltpu.SemaphoreType.DMA((1,)),

time: 149 us -> 148 us (level)
  Pallas kernels: 149 us -> 147 us
where the time goes in v4:
time: 148 us
  Pallas kernels  147 us (99%)
    pallas_call x1, Pallas kernels, body(): pl.pallas_call(functools.partial(kernel, total_rows), out_shape=(pltpu.VM...  144 us
    pallas_call x1, Pallas kernels, body(): pl.pallas_call(deliver, out_shape=(jax.ShapeDtypeStruct((256, 256), F32),...  3.48 us

profile of v4, /device:TPU:1, one launch (start us, length us, event | category | flops | bytes accessed | tf_op | source)
XLA Modules:
  0.0 147.9 jit_solution(15951346421598333612)
XLA Ops:
  0.6 143.8 %regroup_apply_reduce.1 = (f32[256,256]{1,0:T(8,128)S(1)}, f32[256,256]{1,0:T(8,128)S(1)}, bf16[16,8,128,256]{3,2,1,0:T(8,128)(2,1)S(1)}) custom-call(s32[64]{0:T(128)} %part_ref.1, s32[64]{0:T(128)} %slot_ref.1, s32[4,4]{1,0:T(4,128)} %face_ref.1, s32[3,128]{1,0:T(4,128)} %bitcast.5, bf16[64,128,256]{2,1,0:T(8,128)(2,1)} %bitcast.4, ...), custom_call_target="tpu_custom_call" | custom-call | flops 7500000256 | bytes 25000000 | tf_op jit(solution)/shard_map/regroup_apply_reduce/pallas_call | solution.py:424
  144.5 3.5 %deliver.1 = (f32[256,256]{1,0:T(8,128)}, f32[256,256]{1,0:T(8,128)}, bf16[16,8,128,256]{3,2,1,0:T(8,128)(2,1)}) custom-call(f32[256,256]{1,0:T(8,128)S(1)} %get-tuple-element.9.refs_0_, f32[256,256]{1,0:T(8,128)S(1)} %get-tuple-element.10.refs_1_, bf16[16,8,128,256]{3,2,1,0:T(8,128)(2,1)S(1)} %get-tuple-element.11.refs_2_), custom_call_target="tpu_custom_call" | custom-call | bytes 17800000 | tf_op jit(solution)/shard_map/deliver/pallas_call | solution.py:442
